TPU v7x, 32 devices: a whole 2x2x4 slice. The times are simulated.
32 devices in a mesh: dp: 4 (over y, x), ctx: 8 (over z, core).
Axes of the slice: x: 2, y: 2, z: 4, core: 2. Of those that a mesh axis runs over, the one named last changes fastest.
Arguments:
- hidden_in: bfloat16 [8, 1024, 768], P('dp', 'ctx'), may hold values from -6 to 6
- cotangent: bfloat16 [8, 1024, 768], P('dp', 'ctx'), may hold values from -6 to 6
- w_qkv: bfloat16 [768, 2304], P('dp'), may hold values from -0.3125 to 0.3125
- w_out: bfloat16 [768, 768], P('dp'), may hold values from -0.875 to 0.875
- w_in: bfloat16 [768, 2304], P('dp'), may hold values from -0.21875 to 0.21875
- w_mix: bfloat16 [1152, 768], P('dp'), may hold values from -0.25 to 0.25
- attn_gain: bfloat16 [768], P('dp'), may hold values from 0.5 to 1.5
- mlp_gain: bfloat16 [768], P('dp'), may hold values from 0.5 to 1.5
- segment_ids: int32 [8, 1024], P('dp', 'ctx'), may hold values from 0 to 7, as said below
- positions: int32 [8, 1024], P('dp', 'ctx'), may hold values from 0 to 1023, as said below
Outputs:
- output: bfloat16 [8, 1024, 768], P('dp', 'ctx')
- grad_input: bfloat16 [8, 1024, 768], P('dp', 'ctx')
- grad_w_qkv: float32 [768, 2304], P('dp')
- grad_w_out: float32 [768, 768], P('dp')
- grad_w_in: float32 [768, 2304], P('dp')
- grad_w_mix: float32 [1152, 768], P('dp')
- grad_attn_gain: float32 [768], P('dp')
- grad_mlp_gain: float32 [768], P('dp')
Inputs may be any that keep to these rules, and one draw needn't show every extreme that they name: `segment_ids`: along each sequence segment numbers start at 0 and never fall, rising by at most one between neighbouring positions; in each group of 2 sequences of one dp index one sequence is a single document. `positions`: each position's index within its document, counted from 0 at the document's first position.
All inputs are finite; a program needn't handle non-finite values.
Results may differ from a plain program's by a relative error of at most 0.025.
Values may be sent and summed in bfloat16 or wider, within the bound.
A program may use at most 128 MiB of HBM per device.

v0:
```python
import jax
import jax.numpy as jnp
from jax import lax
from jax.sharding import PartitionSpec as P

HEADS = 12
HEAD_DIM = 64


epsilon = 1e-05
rope_base = 160000.0
masked_score = -1e30


def norm_gain(values, gain_row):
    row_mean = jnp.mean(values, -1, keepdims=True)
    centred = values - row_mean
    return centred * lax.rsqrt(jnp.mean(centred * centred, -1, keepdims=True) + epsilon) * gain_row


def rotate(values, positions, direction):
    half_width = values.shape[-1] // 2
    frequency = rope_base ** (-2.0 * jnp.arange(half_width, dtype=jnp.float32) / values.shape[-1])
    angles = positions.astype(jnp.float32)[..., None] * frequency
    cosine = jnp.cos(angles)[..., None, :]
    sine_part = direction * jnp.sin(angles)[..., None, :]
    first_half = values[..., :half_width]
    second = values[..., half_width:]
    return jnp.concatenate(
        [first_half * cosine - second * sine_part, second * cosine + first_half * sine_part], -1
    )


def geglu(projected):
    half_width = projected.shape[-1] // 2
    return jax.nn.gelu(projected[..., :half_width], approximate=False) * projected[..., half_width:]


def inner(left_arg, right_arg):
    return lax.dot_general(
        left_arg, right_arg, (((0,), (0,)), ((), ())), preferred_element_type=jnp.float32
    )


def times_back(left_arg, right_arg):
    return lax.dot_general(
        left_arg, right_arg, (((1,), (1,)), ((), ())), preferred_element_type=jnp.float32
    )


def heads_view(values):
    return values.reshape(values.shape[:2] + (HEADS, HEAD_DIM))


def same_doc(query_docs, key_docs):
    return query_docs[:, None, :, None] == key_docs[:, None, None, :]


def blockwise(stepper, initial, arrays, block_len):
    key_count = arrays[0].shape[1]
    block_count = key_count // block_len
    pieces = tuple(
        (
            jnp.moveaxis(
                member.reshape(member.shape[:1] + (block_count, block_len) + member.shape[2:]), 1, 0
            )
            for member in arrays
        )
    )
    return lax.scan(lambda running, members: (stepper(running, members), None), initial, pieces)[0]


def body(
    hidden_in, cotangent, w_qkv, w_out, w_in, w_mix, attn_gain, mlp_gain, segment_ids, positions
):
    seq_count, local_len, model_width = hidden_in.shape
    row_count = seq_count * local_len
    score_scale = HEAD_DIM ** (-0.5)
    full_qkv, full_out, full_in, full_mix, gain_attn, gain_mlp = (
        lax.all_gather(w_qkv, "dp", axis=0, tiled=True),
        lax.all_gather(w_out, "dp", axis=0, tiled=True),
        lax.all_gather(w_in, "dp", axis=0, tiled=True),
        lax.all_gather(w_mix, "dp", axis=0, tiled=True),
        lax.all_gather(attn_gain, "dp", axis=0, tiled=True),
        lax.all_gather(mlp_gain, "dp", axis=0, tiled=True),
    )
    all_segments = lax.all_gather(segment_ids, "ctx", axis=1, tiled=True)
    inputs = hidden_in.astype(jnp.float32).reshape(row_count, model_width)
    normed_attn, attn_norm_back = jax.vjp(norm_gain, inputs, gain_attn.astype(jnp.float32))
    normed_low = normed_attn.astype(jnp.bfloat16)
    projected = jnp.dot(normed_low, full_qkv, preferred_element_type=jnp.float32).reshape(
        seq_count, local_len, 3, HEADS, HEAD_DIM
    )
    query_heads = rotate(projected[:, :, 0], positions, 1.0).astype(jnp.bfloat16)
    key_low = (
        rotate(projected[:, :, 1], positions, 1.0)
        .astype(jnp.bfloat16)
        .reshape(seq_count, local_len, model_width)
    )
    value_low = projected[:, :, 2].astype(jnp.bfloat16).reshape(seq_count, local_len, model_width)
    key_heads = heads_view(key_low)
    value_heads = heads_view(value_low)

    def attend_block(running, members):
        row_max, row_total, weighted = running
        key_part, value_part, key_docs = members
        scores = (
            jnp.einsum(
                "sqhd,skhd->shqk",
                query_heads,
                heads_view(key_part),
                preferred_element_type=jnp.float32,
            )
            * score_scale
        )
        allowed = same_doc(segment_ids, key_docs)
        newest = jnp.maximum(row_max, jnp.max(jnp.where(allowed, scores, masked_score), -1))
        weights = jnp.where(allowed, jnp.exp(scores - newest[..., None]), 0.0)
        factor = jnp.exp(row_max - newest)
        update = jnp.einsum(
            "shqk,skhd->sqhd",
            weights.astype(jnp.bfloat16),
            heads_view(value_part),
            preferred_element_type=jnp.float32,
        )
        return (
            newest,
            row_total * factor + jnp.sum(weights, -1),
            weighted * jnp.moveaxis(factor, 1, 2)[..., None] + update,
        )

    stat_shape = (seq_count, HEADS, local_len)
    head_shape = (seq_count, local_len, HEADS, HEAD_DIM)
    start_state = (
        jnp.full(stat_shape, masked_score, jnp.float32),
        jnp.zeros(stat_shape, jnp.float32),
        jnp.zeros(head_shape, jnp.float32),
    )
    arriving = (
        lax.all_gather(key_low, "ctx", axis=1, tiled=True),
        lax.all_gather(value_low, "ctx", axis=1, tiled=True),
    )
    key_docs = all_segments
    row_max, row_total, weighted = blockwise(
        attend_block, start_state, (arriving[0], arriving[1], key_docs), local_len
    )
    attention = (weighted / jnp.moveaxis(row_total, 1, 2)[..., None]).reshape(
        row_count, model_width
    )
    log_total = jnp.moveaxis(row_max + jnp.log(row_total), 1, 2)
    attn_low = attention.astype(jnp.bfloat16)
    residual = inputs + jnp.dot(attn_low, full_out, preferred_element_type=jnp.float32)
    normed_mlp, mlp_norm_back = jax.vjp(norm_gain, residual, gain_mlp.astype(jnp.float32))
    mlp_low = normed_mlp.astype(jnp.bfloat16)
    wide_proj = jnp.dot(mlp_low, full_in, preferred_element_type=jnp.float32)
    activated, geglu_back = jax.vjp(geglu, wide_proj)
    act_low = activated.astype(jnp.bfloat16)
    output = residual + jnp.dot(act_low, full_mix, preferred_element_type=jnp.float32)
    grad_out = cotangent.reshape(row_count, model_width)
    grad_mix = inner(act_low, grad_out)
    grad_wide = geglu_back(times_back(grad_out, full_mix))[0].astype(jnp.bfloat16)
    grad_in = inner(mlp_low, grad_wide)
    grad_norm_in, grad_gain_mlp = mlp_norm_back(times_back(grad_wide, full_in))
    grad_resid = grad_out.astype(jnp.float32) + grad_norm_in
    grad_branch = grad_resid.astype(jnp.bfloat16)
    grad_attn_out = inner(attn_low, grad_branch)
    grad_heads = times_back(grad_branch, full_out).astype(jnp.bfloat16)
    grad_view = grad_heads.reshape(head_shape)
    offsets = jnp.sum(grad_view.astype(jnp.float32) * attention.reshape(head_shape), -1)
    all_logs, all_offsets = (
        lax.all_gather(log_total, "ctx", axis=1, tiled=True),
        lax.all_gather(offsets, "ctx", axis=1, tiled=True),
    )
    own_logs = jnp.moveaxis(log_total, 2, 1)[..., None]
    own_offsets = jnp.moveaxis(offsets, 2, 1)[..., None]
    grad_rows = grad_heads.reshape(seq_count, local_len, model_width)
    query_low = query_heads.reshape(seq_count, local_len, model_width)

    def query_terms(key_part, value_part, key_docs):
        scores = (
            jnp.einsum(
                "sqhd,skhd->shqk",
                query_heads,
                heads_view(key_part),
                preferred_element_type=jnp.float32,
            )
            * score_scale
        )
        allowed = same_doc(segment_ids, key_docs)
        attn_probs = jnp.where(allowed, jnp.exp(scores - own_logs), 0.0)
        grad_probs = jnp.einsum(
            "sqhd,skhd->shqk", grad_view, heads_view(value_part), preferred_element_type=jnp.float32
        )
        grad_scores = (attn_probs * (grad_probs - own_offsets)).astype(jnp.bfloat16)
        return (
            jnp.einsum(
                "shqk,skhd->sqhd",
                grad_scores,
                heads_view(key_part),
                preferred_element_type=jnp.float32,
            )
            * score_scale
        )

    def key_terms(query_part, grad_part, query_docs, logs_part, offsets_part):
        query_view = heads_view(query_part)
        grad_part_view = heads_view(grad_part)
        scores = (
            jnp.einsum("sqhd,skhd->shqk", query_view, key_heads, preferred_element_type=jnp.float32)
            * score_scale
        )
        allowed = same_doc(query_docs, segment_ids)
        attn_probs = jnp.where(
            allowed, jnp.exp(scores - jnp.moveaxis(logs_part, 2, 1)[..., None]), 0.0
        )
        grad_value = jnp.einsum(
            "shqk,sqhd->skhd",
            attn_probs.astype(jnp.bfloat16),
            grad_part_view,
            preferred_element_type=jnp.float32,
        )
        grad_probs = jnp.einsum(
            "sqhd,skhd->shqk", grad_part_view, value_heads, preferred_element_type=jnp.float32
        )
        grad_scores = (
            attn_probs * (grad_probs - jnp.moveaxis(offsets_part, 2, 1)[..., None])
        ).astype(jnp.bfloat16)
        grad_key = (
            jnp.einsum(
                "shqk,sqhd->skhd", grad_scores, query_view, preferred_element_type=jnp.float32
            )
            * score_scale
        )
        return (grad_key, grad_value)

    zero_heads = jnp.zeros(head_shape, jnp.float32)

    def query_block(running, members):
        return running + query_terms(members[0], members[1], members[2])

    arriving = (
        lax.all_gather(key_low, "ctx", axis=1, tiled=True),
        lax.all_gather(value_low, "ctx", axis=1, tiled=True),
    )
    grad_query = blockwise(
        query_block, zero_heads, (arriving[0], arriving[1], all_segments), local_len
    )

    def key_block(running, members):
        grad_key, grad_value = key_terms(members[0], members[1], members[2], members[3], members[4])
        return (running[0] + grad_key, running[1] + grad_value)

    grad_key, grad_value = blockwise(
        key_block,
        (zero_heads, zero_heads),
        (
            lax.all_gather(query_low, "ctx", axis=1, tiled=True),
            lax.all_gather(grad_rows, "ctx", axis=1, tiled=True),
        )
        + (all_segments, all_logs, all_offsets),
        local_len,
    )
    grad_qkv = (
        jnp.stack(
            [rotate(grad_query, positions, -1.0), rotate(grad_key, positions, -1.0), grad_value], 2
        )
        .reshape(row_count, 3 * model_width)
        .astype(jnp.bfloat16)
    )
    grad_qkv_w = inner(normed_low, grad_qkv)
    grad_norm_attn, grad_gain_attn = attn_norm_back(times_back(grad_qkv, full_qkv))
    grad_hidden = (grad_resid + grad_norm_attn).astype(jnp.bfloat16).reshape(hidden_in.shape)
    grad_terms = (grad_qkv_w, grad_attn_out, grad_in, grad_mix, grad_gain_attn, grad_gain_mlp)
    summed = (
        lax.psum(grad_terms[0].astype(jnp.bfloat16), "ctx").astype(jnp.float32),
        lax.psum(grad_terms[1].astype(jnp.bfloat16), "ctx").astype(jnp.float32),
        lax.psum(grad_terms[2].astype(jnp.bfloat16), "ctx").astype(jnp.float32),
        lax.psum(grad_terms[3].astype(jnp.bfloat16), "ctx").astype(jnp.float32),
        lax.psum(grad_terms[4].astype(jnp.bfloat16), "ctx").astype(jnp.float32),
        lax.psum(grad_terms[5].astype(jnp.bfloat16), "ctx").astype(jnp.float32),
    )
    owner_grads = (
        lax.psum_scatter(
            summed[0].astype(jnp.bfloat16), "dp", scatter_dimension=0, tiled=True
        ).astype(jnp.float32),
        lax.psum_scatter(
            summed[1].astype(jnp.bfloat16), "dp", scatter_dimension=0, tiled=True
        ).astype(jnp.float32),
        lax.psum_scatter(
            summed[2].astype(jnp.bfloat16), "dp", scatter_dimension=0, tiled=True
        ).astype(jnp.float32),
        lax.psum_scatter(
            summed[3].astype(jnp.bfloat16), "dp", scatter_dimension=0, tiled=True
        ).astype(jnp.float32),
        lax.psum_scatter(
            summed[4].astype(jnp.bfloat16), "dp", scatter_dimension=0, tiled=True
        ).astype(jnp.float32),
        lax.psum_scatter(
            summed[5].astype(jnp.bfloat16), "dp", scatter_dimension=0, tiled=True
        ).astype(jnp.float32),
    )
    return (
        output.astype(jnp.bfloat16).reshape(hidden_in.shape),
        grad_hidden,
        owner_grads[0],
        owner_grads[1],
        owner_grads[2],
        owner_grads[3],
        owner_grads[4],
        owner_grads[5],
    )


def solution(mesh):
    placed = (
        P("dp", "ctx", None),
        P("dp", "ctx", None),
        P("dp", None),
        P("dp", None),
        P("dp", None),
        P("dp", None),
        P("dp"),
        P("dp"),
        P("dp", "ctx"),
        P("dp", "ctx"),
    )
    return jax.shard_map(
        body,
        mesh=mesh,
        in_specs=placed,
        out_specs=(
            P("dp", "ctx", None),
            P("dp", "ctx", None),
            P("dp", None),
            P("dp", None),
            P("dp", None),
            P("dp", None),
            P("dp"),
            P("dp"),
        ),
        check_vma=False,
    )
```

profile of v0, /device:TPU:0, one launch (start us, length us, event | category | flops | bytes accessed | tf_op | source)
XLA Modules:
  0.0 598.2 jit_solution(9342363615535313361)
XLA Ops:
  11.7 11.9 %all-reduce.9 = (bf16[768]{0:T(1024)(128)(2,1)S(1)}, bf16[768]{0:T(1024)(128)(2,1)}) all-reduce(bf16[768]{0:T(1024)(128)(2,1)S(1)} %dynamic-update-slice, bf16[768]{0:T(1024)(128)(2,1)S(1)} %dynamic-update-slice.1), channel_id=1, replica_groups=mesh['dp'=4,'ctx'=8] {'dp'}, use_global_device_ids=true, to_apply=%add.2 | all-reduce | flops 1536 | bytes 6144
  27.6 32.2 %all-gather.9.cloned.1.call-done = bf16[768,2304]{1,0:T(8,128)(2,1)} async-done(((bf16[192,2304]{1,0:T(8,128)(2,1)}), bf16[768,2304]{1,0:T(8,128)(2,1)}) %all-gather.9.cloned.1.call-update) | async-done | bytes 3538960 | tf_op jit(solution)/shard_map/all_gather | solution.py:80
  59.8 4.5 copy.51
  75.5 12.9 %all_gather.41 = s32[2,1024]{1,0:T(2,128)} all-gather(s32[2,128]{1,0:T(2,128)} %param.24), channel_id=1, replica_groups=mesh['dp'=4,'ctx'=8] {'ctx'}, dimensions={1}, use_global_device_ids=true | all-gather | bytes 9216 | tf_op jit(solution)/shard_map/all_gather | solution.py:87
  89.7 19.7 %all-gather.11.cloned.1.call-done = bf16[2,1024,768]{2,1,0:T(8,128)(2,1)} async-done(((bf16[2,128,768]{2,1,0:T(8,128)(2,1)}), bf16[2,1024,768]{2,1,0:T(8,128)(2,1)}) %all-gather.11.cloned.1.call-update) | async-done | bytes 3145744 | tf_op jit(solution)/shard_map/all_gather | solution.py:140
  109.3 4.7 copy.55
  114.0 34.7 %all-gather.13.cloned.1.call-done = bf16[2,1024,768]{2,1,0:T(8,128)(2,1)} async-done(((bf16[2,128,768]{2,1,0:T(8,128)(2,1)}), bf16[2,1024,768]{2,1,0:T(8,128)(2,1)}) %all-gather.13.cloned.1.call-update) | async-done | bytes 3145744 | tf_op jit(solution)/shard_map/all_gather | solution.py:141
  148.7 4.6 copy.56
  153.4 31.0 %while.39 = (s32[]{:T(128)}, f32[2,12,128]{2,1,0:T(8,128)S(1)}, f32[2,12,128]{2,1,0:T(8,128)S(1)}, f32[2,128,12,64]{1,3,2,0:T(8,128)S(1)}, s32[2,128]{1,0:T(2,12...) while((s32[]{:T(128)}, f32[2,12,128]{2,1,0:T(8,128)S(1)}, ...), condition=%wide.region_5.6_spmd.clone, body=%wide.region_2.5_spmd.clone.sunk | while | flops 104843264 | bytes 9375873 | solution.py:70
  189.0 37.0 %all-gather.17.cloned.1.call-done = bf16[768,2304]{1,0:T(8,128)(2,1)} async-done(((bf16[192,2304]{1,0:T(8,128)(2,1)}), bf16[768,2304]{1,0:T(8,128)(2,1)}) %all-gather.17.cloned.1.call-update) | async-done | bytes 3538960 | tf_op jit(solution)/shard_map/all_gather | solution.py:82
  226.0 3.2 fusion.63
  229.2 31.2 %all-gather.19.cloned.1.call-done = bf16[1152,768]{1,0:T(8,128)(2,1)} async-done(((bf16[288,768]{1,0:T(8,128)(2,1)}), bf16[1152,768]{1,0:T(8,128)(2,1)}) %all-gather.19.cloned.1.call-update) | async-done | bytes 1769488 | tf_op jit(solution)/shard_map/all_gather | solution.py:83
  260.3 4.4 fusion.51
  281.6 54.3 %while.40 = (s32[]{:T(128)}, f32[2,128,12,64]{1,3,2,0:T(8,128)}, bf16[8,2,128,768]{2,3,1,0:T(8,128)(2,1)}, s32[2,128]{1,0:T(2,128)}, s32[8,2,128]{2,1,0:T(2,128)...) while((s32[]{:T(128)}, f32[2,128,12,64]{1,3,2,0:T(8,128)}, ...), condition=%wide.region_12.13_spmd.clone, body=%wide.region_11.12_spmd.clone.sunk | while | flops 153976832 | bytes 8351879 | solution.py:70
  291.7 3.1 fusion.140
  298.5 3.1 fusion.140
  305.3 3.1 fusion.140
  312.2 3.1 fusion.140
  319.0 3.2 fusion.140
  325.8 3.2 fusion.140
  332.7 3.1 fusion.140
  335.8 11.9 %all_gather.53 = f32[2,1024,12]{1,0,2:T(2,128)S(1)} all-gather(f32[2,128,12]{1,0,2:T(2,128)S(1)} %copy-done.31), channel_id=1, replica_groups=mesh['dp'=4,'ctx'=8] {'ctx'}, dimensions={1}, use_global_device_ids=true | all-gather | bytes 110592 | tf_op jit(solution)/shard_map/all_gather | solution.py:172
  348.5 14.2 %all_gather.51 = f32[2,1024,12]{1,2,0:T(8,128)S(1)} all-gather(f32[2,128,12]{1,2,0:T(8,128)} %get-tuple-element.469), channel_id=1, replica_groups=mesh['dp'=4,'ctx'=8] {'ctx'}, dimensions={1}, use_global_device_ids=true | all-gather | bytes 110592 | tf_op jit(solution)/shard_map/all_gather | solution.py:171
  363.3 4.7 convolution_convert_fusion
  368.2 94.1 %while.41 = (s32[]{:T(128)}, f32[2,128,12,64]{1,3,2,0:T(8,128)}, f32[2,128,12,64]{1,3,2,0:T(8,128)}, bf16[8,2,128,768]{3,2,0,1:T(8,128)(2,1)}, s32[8,2,128]{2,1,...) while((s32[]{:T(128)}, f32[2,128,12,64]{1,3,2,0:T(8,128)}, ...), condition=%wide.region_14.15_spmd.clone, body=%wide.region_13.14_spmd.clone.sunk | while | flops 205094912 | bytes 15134900 | solution.py:70
  423.1 3.0 fusion.149
  466.4 3.0 convolution_convert_fusion.1
  473.4 41.0 %reduce-scatter.5.cloned.1.call-done = bf16[192,2304]{1,0:T(8,128)(2,1)} async-done(((bf16[768,2304]{1,0:T(8,128)(2,1)}), bf16[192,2304]{1,0:T(8,128)(2,1)}) %reduce-scatter.5.cloned.1.call-update) | async-done | bytes 884752 | tf_op jit(solution)/shard_map/reduce_scatter | solution.py:283
  515.5 3.2 multiply_reduce_fusion.2
  519.4 8.9 %all-reduce.8 = (bf16[768]{0:T(1024)(128)(2,1)S(1)}, bf16[768]{0:T(1024)(128)(2,1)S(1)}) all-reduce(bf16[768]{0:T(1024)(128)(2,1)S(1)} %get-tuple-element.364, bf16[768]{0:T(1024)(128)(2,1)S(1)} %copy-done.45), channel_id=6, replica_groups=mesh['dp'=4,'ctx'=8] {'dp'}, use_global_device_ids=true, to_apply=%region_27.28.clone | all-reduce | flops 1536 | bytes 6144
  528.4 14.8 %all-reduce.6 = (bf16[192]{0:T(256)(128)(2,1)S(1)}, bf16[192]{0:T(256)(128)(2,1)S(1)}) all-reduce(bf16[192]{0:T(256)(128)(2,1)S(1)} %dynamic-slice.3, bf16[192]{0:T(256)(128)(2,1)S(1)} %dynamic-slice.5), channel_id=1, replica_groups=mesh['dp'=4,'ctx'=8] {'ctx'}, use_global_device_ids=true, to_apply=%region_26.27 | all-reduce | flops 384 | bytes 1536 | tf_op jit(solution)/shard_map/psum | solution.py:279
  545.5 40.4 %all-reduce.12.cloned.1.call-done = (bf16[192,2304]{1,0:T(8,128)(2,1)}, bf16[192,768]{1,0:T(8,128)(2,1)}, bf16[192,2304]{1,0:T(8,128)(2,1)}, bf16[288,768]{1,0:T(8,128)(2,1)}) async-done(((bf16[192,2304]{1,0:T(8,128)(2,1)}, bf16[192,768]{1,0:T(8,128)(2,1)}, bf16[192,2304]{1,0:T(8,128)(2,1)}, bf16[288,768]{1,0:T(8,128)(2,1)}), (bf16[192,2304]{1,0:T(8,128)(2,1)}, bf16[192,768]{1,0:T(8,128)(2,1)}, ...) | async-done | bytes 2506768 | tf_op jit(solution)/shard_map/psum | solution.py:275
  (409 shorter events, 212.9 us)
Async XLA Ops:
  7.2 17.1 %copy-start.3 = (bf16[2,128,768]{2,1,0:T(8,128)(2,1)S(1)}, bf16[2,128,768]{2,1,0:T(8,128)(2,1)}, u32[]{:S(2)}) copy-start(bf16[2,128,768]{2,1,0:T(8,128)(2,1)} %param.16) | copy-start | bytes 1179652
  7.2 52.7 %all-gather.9.cloned.1.call-start = ((), (), s32[]{:S(2)}) async-start(), calls=%async_computation.4 | async-start | bytes 4423680 | tf_op jit(solution)/shard_map/all_gather | solution.py:80
  7.9 101.4 %all-gather.11.cloned.1.call-start = ((), (), s32[]{:S(2)}) async-start(), calls=%async_computation.5 | async-start | bytes 3538944 | tf_op jit(solution)/shard_map/all_gather | solution.py:140
  23.6 3.1 copy-start.32
  70.9 77.8 %all-gather.13.cloned.1.call-start = ((), (), s32[]{:S(2)}) async-start(), calls=%async_computation.6 | async-start | bytes 3538944 | tf_op jit(solution)/shard_map/all_gather | solution.py:141
  73.1 113.0 %all-gather.15.cloned.1.call-start = ((), (), s32[]{:S(2)}) async-start(), calls=%async_computation.7 | async-start | bytes 1474560 | tf_op jit(solution)/shard_map/all_gather | solution.py:81
  73.7 152.3 %all-gather.17.cloned.1.call-start = ((), (), s32[]{:S(2)}) async-start(), calls=%async_computation.8 | async-start | bytes 4423680 | tf_op jit(solution)/shard_map/all_gather | solution.py:82
  74.3 186.1 %all-gather.19.cloned.1.call-start = ((), (), s32[]{:S(2)}) async-start(), calls=%async_computation.9 | async-start | bytes 2211840 | tf_op jit(solution)/shard_map/all_gather | solution.py:83
  74.8 293.3 %all-gather.21.cloned.1.call-start = ((), (), s32[]{:S(2)}) async-start(), calls=%async_computation.10 | async-start | bytes 3538944 | tf_op jit(solution)/shard_map/all_gather | solution.py:257
  89.4 278.7 %all-gather.23.cloned.1.call-start = ((), (), s32[]{:S(2)}) async-start(), calls=%async_computation.11 | async-start | bytes 3538944 | tf_op jit(solution)/shard_map/all_gather | solution.py:258
  184.3 3.8 copy-start.22
  264.8 3.1 copy-start.13
  266.3 3.4 copy-start.10
  272.9 200.6 %reduce-scatter.7.cloned.1.call-start = ((), (), s32[]{:S(2)}) async-start(), calls=%async_computation.13 | async-start | bytes 1474560 | tf_op jit(solution)/shard_map/reduce_scatter | solution.py:286
  274.5 199.0 %reduce-scatter.11.cloned.1.call-start = ((), (), s32[]{:S(2)}) async-start(), calls=%async_computation.15 | async-start | bytes 2211840 | tf_op jit(solution)/shard_map/reduce_scatter | solution.py:292
  278.1 3.1 copy-start.30
  281.3 192.2 %reduce-scatter.9.cloned.1.call-start = ((), (), s32[]{:S(2)}) async-start(), calls=%async_computation.14 | async-start | bytes 4423680 | tf_op jit(solution)/shard_map/reduce_scatter | solution.py:289
  281.6 54.3 %copy-start.31 = (f32[2,128,12]{1,0,2:T(2,128)S(1)}, f32[2,128,12]{1,0,2:T(2,128)}, u32[]{:S(2)}) copy-start(f32[2,128,12]{1,0,2:T(2,128)} %copy-done.30) | copy-start | bytes 36868
  281.6 81.8 %copy-start.28 = (f32[768]{0:T(1024)S(1)}, f32[768]{0:T(1024)}, u32[]{:S(2)}) copy-start(f32[768]{0:T(1024)} %convert_element_type.163) | copy-start | bytes 9220
  368.1 146.4 %reduce-scatter.5.cloned.1.call-start = ((), (), s32[]{:S(2)}) async-start(), calls=%async_computation.12 | async-start | bytes 4423680 | tf_op jit(solution)/shard_map/reduce_scatter | solution.py:283
  383.5 3.4 copy-start.2
  395.6 3.4 copy-start.2
  407.7 3.4 copy-start.2
  419.7 3.4 copy-start.2
  431.8 3.4 copy-start.2
  443.9 3.4 copy-start.2
  456.0 3.4 copy-start.2
  469.5 116.4 %all-reduce.12.cloned.1.call-start = ((), (), s32[]{:S(2)}) async-start(), calls=%async_computation.16 | async-start | bytes 5013504 | tf_op jit(solution)/shard_map/psum | solution.py:275
  515.5 3.3 copy-start.43
  518.7 25.6 %copy-start.7 = (f32[256,768]{1,0:T(8,128)S(1)}, f32[256,768]{1,0:T(8,128)}, u32[]{:S(2)}) copy-start(f32[256,768]{1,0:T(8,128)} %copy-done.6) | copy-start | bytes 2359300
  518.7 25.6 %copy-start.15 = (bf16[2,128,768]{2,1,0:T(8,128)(2,1)S(1)}, bf16[2,128,768]{2,1,0:T(8,128)(2,1)}, u32[]{:S(2)}) copy-start(bf16[2,128,768]{2,1,0:T(8,128)(2,1)} %param.17) | copy-start | bytes 1179652
  518.7 25.6 %copy-start.39 = (f32[256]{0:T(256)S(1)}, f32[256]{0:T(256)}, u32[]{:S(2)}) copy-start(f32[256]{0:T(256)} %copy-done.38) | copy-start | bytes 3076
  (34 other events, 53.8 us)
Sparse Core Ops, SparseCore 0:
  9.9 49.9 all-gather.8
  71.0 38.2 all-gather.10
  111.5 37.1 all-gather.12
  150.4 26.5 all-gather.14
  178.7 47.2 all-gather.16
  227.7 32.5 all-gather.18
  261.9 38.2 all-gather.20
  301.9 37.1 all-gather.22
  342.5 27.4 reduce-scatter.6
  373.4 32.4 reduce-scatter.10
  409.0 47.2 reduce-scatter.8
  469.6 44.8 reduce-scatter.4
  517.1 68.7 all-reduce.11
where the time goes:
time: 602 us; the launch traced here: 598 us
  waiting for transfers between devices  239 us (40%)
  matrix products  122 us (20%)
  local copies, waits for them, and re-layouts  98.1 us (16%)
  blocking collectives  74.6 us (12%)
  other arithmetic  47 us (8%)
  between operations  15.8 us (3%)
    dynamic_slice x72, local copies, waits for them, and re-layouts, blockwise(): lax.scan(lambda running, members: (stepper(running, members), None), init...  46.5 us
    reduce_scatter x1, waiting for transfers between devices, body(): lax.psum_scatter(summed[0].astype(jnp.bfloat16), 'dp', scatter_dimension=...  41 us
    psum x1, waiting for transfers between devices, body(): lax.psum(grad_terms[0].astype(jnp.bfloat16), 'ctx').astype(jnp.float32)  40.4 us
    all_gather x1, waiting for transfers between devices, body(): lax.all_gather(w_in, 'dp', axis=0, tiled=True)  37 us
    all_gather x1, waiting for transfers between devices, body(): lax.all_gather(value_low, 'ctx', axis=1, tiled=True)  34.7 us
    all_gather x1, waiting for transfers between devices, body(): lax.all_gather(w_qkv, 'dp', axis=0, tiled=True)  32.2 us
    all_gather x1, waiting for transfers between devices, body(): lax.all_gather(w_mix, 'dp', axis=0, tiled=True)  31.2 us
    dot_general x8, matrix products, query_terms(): jnp.einsum('shqk,skhd->sqhd', grad_scores, heads_view(key_part), preferre...  24.9 us
  transfers between devices with their start and end apart: 13, of which 7 were waited for; matrix products, arithmetic and copies ran while one was open for 41% of the time, Pallas kernels for 0%

commit v1 on v0

--- a/solution.py
+++ b/solution.py
@@ -1,6 +1,8 @@
 import jax
 import jax.numpy as jnp
 from jax import lax
+from jax.experimental import pallas as pl
+from jax.experimental.pallas import tpu as pltpu
 from jax.sharding import PartitionSpec as P
 
 HEADS = 12
@@ -70,7 +72,7 @@
     return lax.scan(lambda running, members: (stepper(running, members), None), initial, pieces)[0]
 
 
-def body(
+def long_body(
     hidden_in, cotangent, w_qkv, w_out, w_in, w_mix, attn_gain, mlp_gain, segment_ids, positions
 ):
     seq_count, local_len, model_width = hidden_in.shape
@@ -310,6 +312,500 @@
         owner_grads[5],
     )
 
+PAIR = 2 * HEAD_DIM
+VMEM_LIMIT = 56 * 1024 * 1024
+
+
+def dot_nn(left, right):
+    return jnp.dot(left, right, preferred_element_type=jnp.float32)
+
+
+def turn(values, cosine, sine):
+    lane = lax.broadcasted_iota(jnp.int32, values.shape, 1)
+    half = HEAD_DIM // 2
+    partner = jnp.where(
+        lane % HEAD_DIM < half,
+        pltpu.roll(values, PAIR - half, 1),
+        pltpu.roll(values, half, 1),
+    )
+    return values * cosine + partner * sine
+
+
+def head_lanes(shape, head):
+    lane = lax.broadcasted_iota(jnp.int32, shape, 1)
+    return lane // HEAD_DIM == head
+
+
+def forward_kernel(
+    seqs, x_all, x_own, wq, wk, wv, cos_all, sin_all, cos_own, sin_own, seg_col, seg_row,
+    q_out, k_out, v_out, attn_out, log_out,
+):
+    scale = HEAD_DIM ** (-0.5)
+    q_out[...] = turn(dot_nn(x_own[...], wq[...]), cos_own[...], sin_own[...]).astype(jnp.bfloat16)
+    k_out[...] = turn(dot_nn(x_all[...], wk[...]), cos_all[...], sin_all[...]).astype(jnp.bfloat16)
+    v_out[...] = dot_nn(x_all[...], wv[...]).astype(jnp.bfloat16)
+    local = x_own.shape[0] // seqs
+    length = x_all.shape[0] // seqs
+    for seq in range(seqs):
+        own = pl.ds(seq * local, local)
+        whole = pl.ds(seq * length, length)
+        allowed = seg_col[own, 0:1] == seg_row[seq : seq + 1, :]
+        query, key, value = q_out[own, :], k_out[whole, :], v_out[whole, :]
+        first = head_lanes(query.shape, 0)
+        parts, logs = [], []
+        for head in range(2):
+            picked = jnp.where(head_lanes(query.shape, head), query * scale, 0).astype(jnp.bfloat16)
+            scores = jnp.where(allowed, times_back(picked, key), masked_score)
+            top = jnp.max(scores, -1, keepdims=True)
+            weights = jnp.exp(scores - top)
+            total = jnp.sum(weights, -1, keepdims=True)
+            parts.append(dot_nn(weights.astype(jnp.bfloat16), value) / total)
+            logs.append(top + jnp.log(total))
+        attn_out[own, :] = jnp.where(first, parts[0], parts[1])
+        log_out[own, :] = jnp.where(first, logs[0], logs[1])
+
+
+def backward_kernel(
+    seqs, x_all, x_own, wq, wk, wv, cos_all, sin_all, cos_own, sin_own, seg_col, seg_row,
+    q_own, k_own, v_own, k_all, v_all, g_own, g_all, attn, logs, log_row, off_row,
+    dw_out, r_out, q_all, gp,
+):
+    scale = HEAD_DIM ** (-0.5)
+    q_all[...] = turn(dot_nn(x_all[...], wq[...]), cos_all[...], sin_all[...]).astype(jnp.bfloat16)
+    local = x_own.shape[0] // seqs
+    length = x_all.shape[0] // seqs
+    for seq in range(seqs):
+        own = pl.ds(seq * local, local)
+        whole = pl.ds(seq * length, length)
+        allowed = seg_col[own, 0:1] == seg_row[seq : seq + 1, :]
+        query, key, value, grad = q_own[own, :], k_own[own, :], v_own[own, :], g_own[own, :]
+        query_w, key_w, value_w, grad_w = q_all[whole, :], k_all[whole, :], v_all[whole, :], g_all[whole, :]
+        first = head_lanes(query.shape, 0)
+        weighted = grad.astype(jnp.float32) * attn[own, :]
+        dq, dk, dv = [], [], []
+        for head in range(2):
+            mine = head_lanes(query.shape, head)
+            offset = jnp.sum(jnp.where(mine, weighted, 0.0), -1, keepdims=True)
+            log = logs[own, head * HEAD_DIM : head * HEAD_DIM + 1]
+            picked = jnp.where(mine, query * scale, 0).astype(jnp.bfloat16)
+            scores = times_back(picked, key_w)
+            probs = jnp.exp(jnp.where(allowed, scores - log, masked_score))
+            g_probs = times_back(jnp.where(mine, grad, 0).astype(jnp.bfloat16), value_w)
+            g_scores = (probs * (g_probs - offset)).astype(jnp.bfloat16)
+            dq.append(dot_nn(g_scores, key_w))
+            row = 2 * seq + head
+            picked = jnp.where(mine, key * scale, 0).astype(jnp.bfloat16)
+            scores = times_back(picked, query_w)
+            probs = jnp.exp(jnp.where(allowed, scores - log_row[0, row : row + 1, :], masked_score))
+            dv.append(dot_nn(probs.astype(jnp.bfloat16), grad_w))
+            g_probs = times_back(jnp.where(mine, value, 0).astype(jnp.bfloat16), grad_w)
+            g_scores = (probs * (g_probs - off_row[0, row : row + 1, :])).astype(jnp.bfloat16)
+            dk.append(dot_nn(g_scores, query_w))
+        cosine, sine = cos_own[own, :], -sin_own[own, :]
+        gp[0, own, :] = turn(jnp.where(first, dq[0], dq[1]) * scale, cosine, sine).astype(jnp.bfloat16)
+        gp[1, own, :] = turn(jnp.where(first, dk[0], dk[1]) * scale, cosine, sine).astype(jnp.bfloat16)
+        gp[2, own, :] = jnp.where(first, dv[0], dv[1]).astype(jnp.bfloat16)
+    for part in range(3):
+        dw_out[part] = inner(x_own[...], gp[part]).astype(jnp.bfloat16)
+    back = times_back(gp[0], wq[...]) + times_back(gp[1], wk[...]) + times_back(gp[2], wv[...])
+
+    @pl.when(pl.program_id(0) == 0)
+    def _():
+        r_out[...] = back
+
+    @pl.when(pl.program_id(0) > 0)
+    def _():
+        r_out[...] += back
+
+
+MESH = pl.DeviceIdType.MESH
+
+
+def partner_of(index, step):
+    low = (index % 2 + step % 2) % 2
+    high = (index // 2 + step // 2) % 2
+    return high * 2 + low
+
+
+def meet(peers):
+    barrier = pltpu.get_barrier_semaphore()
+    for peer in peers:
+        pl.semaphore_signal(barrier, inc=1, device_id=peer, device_id_type=MESH)
+    pl.semaphore_wait(barrier, len(peers))
+
+
+def neighbours():
+    dp, ctx = lax.axis_index("dp"), lax.axis_index("ctx")
+    chip, core = ctx // 2, ctx % 2
+    across = [(partner_of(dp, step), ctx) for step in (1, 2, 3)]
+    along = [(dp, partner_of(chip, step) * 2 + core) for step in (1, 2, 3)]
+    return dp, ctx, across, along, (dp, chip * 2 + 1 - core)
+
+
+def gather_kernel(n_dp, n_ctx, *refs):
+    count = n_dp + n_ctx
+    ins, outs = refs[:count], refs[count : 2 * count]
+    own_sem, send, recv, pass_send, pass_recv = refs[2 * count :]
+    dp, ctx, across, along, sibling = neighbours()
+    core = ctx % 2
+    meet((across if n_dp else []) + along + [sibling])
+
+    def part(which, place_dp, place_ctx):
+        out, block = outs[which], ins[which].shape
+        if which < n_dp:
+            half = block[0] // 2
+            return out.at[pl.ds(place_dp * block[0] + core * half, half)]
+        return out.at[:, pl.ds(place_ctx * block[1], block[1])]
+
+    jobs, local = [], []
+    for which in range(count):
+        rows = ins[which].shape[0]
+        peers = across if which < n_dp else along
+        if which < n_dp:
+            source = ins[which].at[pl.ds(core * (rows // 2), rows // 2)]
+            own = outs[which].at[pl.ds(dp * rows, rows)]
+        else:
+            source, own = ins[which], part(which, dp, ctx)
+        keep = pltpu.make_async_copy(ins[which], own, own_sem.at[which])
+        keep.start()
+        local.append(keep)
+        for step in range(3):
+            job = pltpu.make_async_remote_copy(
+                source, part(which, dp, ctx), send.at[which, step], recv.at[which, step],
+                device_id=peers[step], device_id_type=MESH,
+            )
+            job.start()
+            jobs.append((which, step, peers[step], job))
+    passed = []
+    for which in range(n_dp, count):
+        job = pltpu.make_async_remote_copy(
+            ins[which], part(which, dp, ctx), pass_send.at[which, 3], pass_recv.at[which, 3],
+            device_id=sibling, device_id_type=MESH,
+        )
+        job.start()
+        passed.append(job)
+    for which, step, peer, job in jobs:
+        job.wait_recv()
+        landed = part(which, peer[0], peer[1])
+        onward = pltpu.make_async_remote_copy(
+            landed, landed, pass_send.at[which, step], pass_recv.at[which, step],
+            device_id=sibling, device_id_type=MESH,
+        )
+        onward.start()
+        passed.append(onward)
+    for keep in local:
+        keep.wait()
+    for job in jobs:
+        job[3].wait_send()
+    for job in passed:
+        job.wait()
+
+
+def gather(dp_arrays, ctx_arrays, collective):
+    arrays = tuple(dp_arrays) + tuple(ctx_arrays)
+    n_dp, count = len(dp_arrays), len(arrays)
+    dp_size, ctx_size = lax.axis_size("dp"), lax.axis_size("ctx")
+    shapes = [(a.shape[0] * dp_size,) + a.shape[1:] for a in dp_arrays]
+    shapes += [(a.shape[0], a.shape[1] * ctx_size) + a.shape[2:] for a in ctx_arrays]
+    dma = pltpu.SemaphoreType.DMA
+    return pl.pallas_call(
+        lambda *refs: gather_kernel(n_dp, count - n_dp, *refs),
+        in_specs=[pl.BlockSpec(memory_space=pl.ANY)] * count,
+        out_specs=[pl.BlockSpec(memory_space=pl.ANY)] * count,
+        out_shape=[jax.ShapeDtypeStruct(shape, a.dtype) for shape, a in zip(shapes, arrays)],
+        scratch_shapes=[dma((count,)), dma((count, 3)), dma((count, 3)), dma((count, 4)), dma((count, 4))],
+        compiler_params=pltpu.CompilerParams(collective_id=collective, has_side_effects=True),
+    )(*arrays)
+
+
+def reduce_kernel(
+    terms, out, from_core, summed, from_dp, reduced, from_ctx, final,
+    core_send, core_recv, dp_send, dp_recv, ctx_send, ctx_recv, spread_send, spread_recv, last,
+):
+    dp, ctx, across, along, sibling = neighbours()
+    chip, core = ctx // 2, ctx % 2
+    half, width = reduced.shape
+    piece = half // 4
+    meet(across + along + [sibling])
+
+    def add(target, sources):
+        def chunk(index, carry):
+            rows = pl.ds(pl.multiple_of(index * 16, 16), 16)
+            value = sources[0][rows, :].astype(jnp.float32)
+            for source in sources[1:]:
+                value = value + source[rows, :].astype(jnp.float32)
+            target[rows, :] = value.astype(jnp.bfloat16)
+            return carry
+
+        lax.fori_loop(0, target.shape[0] // 16, chunk, 0)
+
+    swaps = []
+    for step in (1, 2, 3, 0):
+        owner = partner_of(dp, step)
+        swap = pltpu.make_async_remote_copy(
+            terms.at[owner, pl.ds((1 - core) * half, half)], from_core.at[step],
+            core_send.at[step], core_recv.at[step], device_id=sibling, device_id_type=MESH,
+        )
+        swap.start()
+        swaps.append(swap)
+    moves = []
+    for step, swap in zip((1, 2, 3, 0), swaps):
+        swap.wait_recv()
+        owner = partner_of(dp, step)
+        add(summed.at[step], [terms.at[owner, pl.ds(core * half, half)], from_core.at[step]])
+        if step:
+            move = pltpu.make_async_remote_copy(
+                summed.at[step], from_dp.at[step - 1], dp_send.at[step - 1], dp_recv.at[step - 1],
+                device_id=across[step - 1], device_id_type=MESH,
+            )
+            move.start()
+            moves.append(move)
+    for move in moves:
+        move.wait_recv()
+    add(reduced, [summed.at[0], from_dp.at[0], from_dp.at[1], from_dp.at[2]])
+    for step in range(3):
+        target = along[step][1] // 2
+        move = pltpu.make_async_remote_copy(
+            reduced.at[pl.ds(target * piece, piece)], from_ctx.at[step], ctx_send.at[step], ctx_recv.at[step],
+            device_id=along[step], device_id_type=MESH,
+        )
+        move.start()
+        moves.append(move)
+    for move in moves[3:]:
+        move.wait_recv()
+    mine = pl.ds(core * half + chip * piece, piece)
+    add(final, [reduced.at[pl.ds(chip * piece, piece)], from_ctx.at[0], from_ctx.at[1], from_ctx.at[2]])
+    spread = []
+    for step in range(3):
+        move = pltpu.make_async_remote_copy(
+            final, out.at[mine], spread_send.at[step], spread_recv.at[step],
+            device_id=along[step], device_id_type=MESH,
+        )
+        move.start()
+        spread.append(move)
+    keep = pltpu.make_async_copy(final, out.at[mine], last.at[0])
+    keep.start()
+    keep.wait()
+    for move in spread:
+        move.wait_recv()
+    whole = pl.ds(core * half, half)
+    share = pltpu.make_async_remote_copy(
+        out.at[whole], out.at[whole], last.at[1], last.at[2], device_id=sibling, device_id_type=MESH
+    )
+    share.start()
+    for move in swaps + moves + spread:
+        move.wait_send()
+    share.wait()
+
+
+def reduce_terms(terms, collective):
+    _, rows, width = terms.shape
+    half = rows // 2
+    bf, dma = jnp.bfloat16, pltpu.SemaphoreType.DMA
+    return pl.pallas_call(
+        reduce_kernel,
+        in_specs=[pl.BlockSpec(memory_space=pltpu.VMEM)],
+        out_specs=pl.BlockSpec(memory_space=pltpu.VMEM),
+        out_shape=jax.ShapeDtypeStruct((rows, width), bf),
+        scratch_shapes=[
+            pltpu.VMEM((4, half, width), bf), pltpu.VMEM((4, half, width), bf), pltpu.VMEM((3, half, width), bf),
+            pltpu.VMEM((half, width), bf), pltpu.VMEM((3, half // 4, width), bf), pltpu.VMEM((half // 4, width), bf),
+            dma((4,)), dma((4,)), dma((3,)), dma((3,)), dma((3,)), dma((3,)), dma((3,)), dma((3,)), dma((3,)),
+        ],
+        compiler_params=pltpu.CompilerParams(
+            collective_id=collective, has_side_effects=True, vmem_limit_bytes=VMEM_LIMIT
+        ),
+    )(terms)
+
+
+def tables(positions):
+    half = HEAD_DIM // 2
+    frequency = rope_base ** (-2.0 * jnp.arange(half, dtype=jnp.float32) / HEAD_DIM)
+    angles = positions.astype(jnp.float32).reshape(-1, 1) * frequency
+    cosine, sine = jnp.cos(angles), jnp.sin(angles)
+    return (
+        jnp.concatenate([cosine] * 4, -1),
+        jnp.concatenate([-sine, sine, -sine, sine], -1),
+    )
+
+
+def body(
+    hidden_in, cotangent, w_qkv, w_out, w_in, w_mix, attn_gain, mlp_gain, segment_ids, positions
+):
+    seqs, local, width = hidden_in.shape
+    rows = seqs * local
+    length = local * lax.axis_size("ctx")
+    total = seqs * length
+    pairs = HEADS // 2
+    bf, f32 = jnp.bfloat16, jnp.float32
+    place = lax.axis_index("ctx") * local
+
+    dp_size, ctx_size = lax.axis_size("dp"), lax.axis_size("ctx")
+    shard = width // dp_size
+    own_gains = jnp.pad(jnp.stack([attn_gain, mlp_gain]), ((0, 30), (0, 256 - shard)))
+    own_marks = jnp.pad(jnp.concatenate([segment_ids, positions]), ((0, 8 - 2 * seqs), (0, 0)))
+    full_qkv, full_out, full_in, full_mix, gains, hidden_all, marks = gather(
+        [w_qkv, w_out, w_in, w_mix, own_gains], [hidden_in, own_marks.reshape(1, 8, local)], 0
+    )
+    gains = gains.reshape(dp_size, 32, 256)[:, :2, :shard]
+    gains = jnp.transpose(gains, (1, 0, 2)).reshape(2, width)
+    marks = marks.reshape(ctx_size, 8, local)[:, : 2 * seqs].reshape(ctx_size, 2, seqs, local)
+    marks = jnp.transpose(marks, (1, 2, 0, 3)).reshape(2, seqs, length)
+    gain_attn, gain_mlp = gains[0].astype(f32), gains[1].astype(f32)
+
+    cos_all, sin_all = tables(marks[1])
+    cos_own, sin_own = tables(positions)
+    seg_row = marks[0]
+    seg_col = jnp.broadcast_to(segment_ids.reshape(rows, 1), (rows, 128))
+
+    inputs = hidden_in.astype(f32).reshape(rows, width)
+    normed_attn, attn_norm_back = jax.vjp(norm_gain, inputs, gain_attn)
+    x_own = normed_attn.astype(bf)
+    x_all = norm_gain(hidden_all.astype(f32).reshape(total, width), gain_attn).astype(bf)
+
+    def const(*shape):
+        return pl.BlockSpec(shape, lambda pair: (0,) * len(shape))
+
+    def column(height, offset=0):
+        return pl.BlockSpec((height, PAIR), lambda pair: (0, pair + offset))
+
+    shared = [
+        const(total, width), const(rows, width),
+        column(width), column(width, pairs), column(width, 2 * pairs),
+        const(total, PAIR), const(total, PAIR), const(rows, PAIR), const(rows, PAIR),
+        const(rows, 128), const(seqs, length),
+    ]
+    shared_args = (
+        x_all, x_own, full_qkv, full_qkv, full_qkv, cos_all, sin_all, cos_own, sin_own, seg_col, seg_row
+    )
+    params = pltpu.CompilerParams(vmem_limit_bytes=VMEM_LIMIT)
+    score_flops = 2 * rows * length * PAIR * HEADS
+    q_own, k_all, v_all, attention, logs = pl.pallas_call(
+        lambda *refs: forward_kernel(seqs, *refs),
+        grid=(pairs,),
+        in_specs=shared,
+        out_specs=[column(rows), column(total), column(total), column(rows), column(rows)],
+        out_shape=[
+            jax.ShapeDtypeStruct((rows, width), bf),
+            jax.ShapeDtypeStruct((total, width), bf),
+            jax.ShapeDtypeStruct((total, width), bf),
+            jax.ShapeDtypeStruct((rows, width), f32),
+            jax.ShapeDtypeStruct((rows, width), f32),
+        ],
+        compiler_params=params,
+        cost_estimate=pl.CostEstimate(
+            flops=2 * score_flops + 4 * total * width * width,
+            bytes_accessed=20 * 1024 * 1024, transcendentals=rows * length * HEADS,
+        ),
+    )(*shared_args)
+
+    attn_low = attention.astype(bf)
+    residual = inputs + dot_nn(attn_low, full_out)
+    normed_mlp, mlp_norm_back = jax.vjp(norm_gain, residual, gain_mlp)
+    mlp_low = normed_mlp.astype(bf)
+    wide_proj = dot_nn(mlp_low, full_in)
+    activated, geglu_back = jax.vjp(geglu, wide_proj)
+    act_low = activated.astype(bf)
+    output = residual + dot_nn(act_low, full_mix)
+    grad_out = cotangent.reshape(rows, width)
+    grad_mix = inner(act_low, grad_out).astype(bf)
+    grad_wide = geglu_back(times_back(grad_out, full_mix))[0].astype(bf)
+    grad_in = inner(mlp_low, grad_wide).astype(bf)
+    grad_norm_in, grad_gain_mlp = mlp_norm_back(times_back(grad_wide, full_in))
+    grad_resid = grad_out.astype(f32) + grad_norm_in
+    grad_branch = grad_resid.astype(bf)
+    grad_attn_out = inner(attn_low, grad_branch).astype(bf)
+    g_own = times_back(grad_branch, full_out).astype(bf)
+
+    feature = lax.broadcasted_iota(jnp.int32, (width, HEADS), 0)
+    head = lax.broadcasted_iota(jnp.int32, (width, HEADS), 1)
+    members = (feature // HEAD_DIM == head).astype(f32)
+    opening = (feature == head * HEAD_DIM).astype(f32)
+    highest = lax.Precision.HIGHEST
+    stats = jnp.concatenate(
+        [
+            jnp.dot(logs, opening, precision=highest),
+            jnp.dot(g_own.astype(f32) * attention, members, precision=highest),
+        ],
+        -1,
+    )
+    upper = lax.reduce_precision(stats, 8, 7)
+    middle = lax.reduce_precision(stats - upper, 8, 7)
+    lower = stats - upper - middle
+    packed = jnp.concatenate(
+        [g_own, upper.astype(bf), middle.astype(bf), lower.astype(bf), jnp.zeros((rows, 128 - 6 * HEADS), bf)], -1
+    )
+    (arrived,) = gather([], [packed.reshape(seqs, local, width + 128)], 1)
+    pieces = arrived[..., width : width + 6 * HEADS].astype(f32)
+    pieces = pieces[..., : 2 * HEADS] + pieces[..., 2 * HEADS : 4 * HEADS] + pieces[..., 4 * HEADS :]
+    rows_view = jnp.transpose(pieces.reshape(seqs, length, 2, pairs, 2), (2, 3, 0, 4, 1)).reshape(
+        2, pairs, 2 * seqs, length
+    )
+    k_own = lax.dynamic_slice(k_all.reshape(seqs, length, width), (0, place, 0), (seqs, local, width))
+    v_own = lax.dynamic_slice(v_all.reshape(seqs, length, width), (0, place, 0), (seqs, local, width))
+    stat_spec = pl.BlockSpec((1, 2 * seqs, length), lambda pair: (pair, 0, 0))
+    dw_qkv, back = pl.pallas_call(
+        lambda *refs: backward_kernel(seqs, *refs),
+        grid=(pairs,),
+        in_specs=shared
+        + [column(rows)] * 3
+        + [column(total)] * 2
+        + [column(rows), column(total), column(rows), column(rows), stat_spec, stat_spec],
+        out_specs=[
+            pl.BlockSpec((3, width, PAIR), lambda pair: (0, 0, pair)),
+            const(rows, width),
+        ],
+        out_shape=[
+            jax.ShapeDtypeStruct((3, width, width), bf),
+            jax.ShapeDtypeStruct((rows, width), f32),
+        ],
+        scratch_shapes=[pltpu.VMEM((total, PAIR), bf), pltpu.VMEM((3, rows, PAIR), bf)],
+        compiler_params=params,
+        cost_estimate=pl.CostEstimate(
+            flops=7 * score_flops + 2 * total * width * width + 12 * rows * width * width,
+            bytes_accessed=25 * 1024 * 1024, transcendentals=2 * rows * length * HEADS,
+        ),
+    )(
+        *shared_args, q_own, k_own.reshape(rows, width), v_own.reshape(rows, width), k_all, v_all,
+        g_own, arrived.reshape(total, width + 128), attention, logs, rows_view[0], rows_view[1],
+    )
+    grad_norm_attn, grad_gain_attn = attn_norm_back(back)
+    grad_hidden = (grad_resid + grad_norm_attn).astype(bf).reshape(hidden_in.shape)
+
+    def by_owner(term):
+        return term.reshape(dp_size, -1, width)
+
+    def thirds(term):
+        parts = [by_owner(term[..., part * width : (part + 1) * width]) for part in range(3)]
+        return parts
+
+    gain_rows = jnp.stack([grad_gain_attn, grad_gain_mlp]).reshape(2, dp_size, shard)
+    gain_rows = jnp.pad(jnp.transpose(gain_rows, (1, 0, 2)), ((0, 0), (0, 0), (0, width - shard)))
+    stacked = [by_owner(dw_qkv[part]) for part in range(3)] + thirds(grad_in)
+    stacked += [by_owner(grad_attn_out), by_owner(grad_mix)]
+    used = sum(term.shape[1] for term in stacked)
+    padded = -(-(used + 2) // 128) * 128
+    stacked.append(jnp.pad(gain_rows.astype(bf), ((0, 0), (0, padded - used - 2), (0, 0))))
+    summed = reduce_terms(jnp.concatenate(stacked, 1), 2).astype(f32)
+    cuts = [summed[part * shard : (part + 1) * shard] for part in range(7)]
+    return (
+        output.astype(bf).reshape(hidden_in.shape),
+        grad_hidden,
+        jnp.concatenate(cuts[:3], 1),
+        cuts[6],
+        jnp.concatenate(cuts[3:6], 1),
+        summed[7 * shard : used],
+        summed[used, :shard],
+        summed[used + 1, :shard],
+    )
+
+
+def layer(hidden_in, *others):
+    sizes = (lax.axis_size("dp"), lax.axis_size("ctx"))
+    if sizes != (4, 8) or hidden_in.shape[0] * hidden_in.shape[1] * sizes[1] > 4096:
+        return long_body(hidden_in, *others)
+    return body(hidden_in, *others)
+
 
 def solution(mesh):
     placed = (
@@ -325,7 +821,7 @@
         P("dp", "ctx"),
     )
     return jax.shard_map(
-        body,
+        layer,
         mesh=mesh,
         in_specs=placed,
         out_specs=(

time: 602 us -> 413 us (0.69)
  Pallas kernels: 0 us -> 327 us
  waiting for transfers between devices: 239 us -> 0 us
  matrix products: 122 us -> 15.3 us
  blocking collectives: 74.6 us -> 0 us
  local copies, waits for them, and re-layouts: 98.1 us -> 35.9 us
  other arithmetic: 47 us -> 28.6 us
  between operations: 15.8 us -> 1.13 us
    pallas_call x0 -> x5, Pallas kernels: none -> 327 us  [the longest x2 133 us: gather(): pl.pallas_call(lambda *refs: gather_kernel(n_dp, count - n_dp, *refs), in...]
    all_gather x8 -> x0, waiting for transfers between devices: 155 us -> none  [the longest x1 37 us: body(): lax.all_gather(w_in, 'dp', axis=0, tiled=True)]
    dot_general x60 -> x5, matrix products: 100 us -> 7.79 us  [the longest x3 6.41 us: dot_nn(): return jnp.dot(left, right, preferred_element_type=jnp.float32)]
    dynamic_slice x72 -> x2, local copies, waits for them, and re-layouts: 46.5 us -> 3.63 us  [the longest x1 1.86 us: body(): lax.dynamic_slice(v_all.reshape(seqs, length, width), (0, place, 0), (seq...]
    reduce_scatter x4 -> x0, waiting for transfers between devices: 41 us -> none  [the longest x1 41 us: body(): lax.psum_scatter(summed[0].astype(jnp.bfloat16), 'dp', scatter_dimension=...]
    psum x1 -> x0, waiting for transfers between devices: 40.4 us -> none  [body(): lax.psum(grad_terms[0].astype(jnp.bfloat16), 'ctx').astype(jnp.float32)]
    all_gather x3 -> x0, blocking collectives: 39 us -> none  [the longest x1 14.2 us: body(): lax.all_gather(log_total, 'ctx', axis=1, tiled=True)]
    eq x24 -> x0, other arithmetic: 23.6 us -> none  [same_doc(): return query_docs[:, None, :, None] == key_docs[:, None, None, :]]
  transfers between devices with their start and end apart: 13 -> 0, of which waited for: 7 -> 0; matrix products, arithmetic and copies ran while one was open for 41% -> 0% of each run, Pallas kernels for 0% -> 0%
where the time goes in v1:
time: 413 us; the launch traced here: 408 us
  Pallas kernels  327 us (79%)
  local copies, waits for them, and re-layouts  35.9 us (9%)
  other arithmetic  28.6 us (7%)
  matrix products  15.3 us (4%)
    pallas_call x2, Pallas kernels, gather(): pl.pallas_call(lambda *refs: gather_kernel(n_dp, count - n_dp, *refs), in...  133 us
    pallas_call x1, Pallas kernels, reduce_terms(): pl.pallas_call(reduce_kernel, in_specs=[pl.BlockSpec(memory_space=pltpu.V...  132 us
    pallas_call x1, Pallas kernels, body(): pl.pallas_call(lambda *refs: backward_kernel(seqs, *refs), grid=(pairs,),...  37.6 us
    pallas_call x1, Pallas kernels, body(): pl.pallas_call(lambda *refs: forward_kernel(seqs, *refs), grid=(pairs,),...  24.4 us
    unnamed x67, local copies, waits for them, and re-layouts  14.1 us

profile of v1, /device:TPU:0, one launch (start us, length us, event | category | flops | bytes accessed | tf_op | source)
XLA Modules:
  0.0 407.7 jit_solution(13444488908635886269)
XLA Ops:
  3.9 95.7 %shard_map.161 = (bf16[768,2304]{1,0:T(8,128)(2,1)}, bf16[768,768]{1,0:T(8,128)(2,1)}, bf16[768,2304]{1,0:T(8,128)(2,1)}, bf16[1152,768]{1,0:T(8,128)(2,1)}, bf1...) custom-call(bf16[192,2304]{1,0:T(8,128)(2,1)} %refs_0_.1, bf16[192,768]{1,0:T(8,128)(2,1)} %refs_1_.1, ...), custom_call_target="tpu_custom_call" | custom-call | tf_op jit(solution)/shard_map/pallas_call | solution.py:511
  100.4 2.5 convert_reduce_fusion
  104.3 2.5 fusion.2.refs_0_
  108.3 3.7 fusion.17
  112.1 3.0 pad_maximum_fusion.2
  117.9 24.4 %shard_map.162 = (bf16[256,768]{1,0:T(8,128)(2,1)}, bf16[2048,768]{1,0:T(8,128)(2,1)}, bf16[2048,768]{1,0:T(8,128)(2,1)}, f32[256,768]{1,0:T(8,128)}, f32[256,768]{1,0:T(8,128)}) custom-call(bf16[2048,768]{1,0:T(8,128)(2,1)} %fusion.2.refs_0_, bf16[256,768]{1,0:T(8,128)(2,1)} %multiply_convert_fusion.2.refs_1_, ...), custom_call_target="tpu_custom_call" | custom-call | flops 6442450944 | bytes 20971520 | tf_op jit(solution)/shard_map/pallas_call | solution.py:683
  142.3 1.7 fusion.54
  144.4 3.3 fusion.45
  147.7 2.8 fusion.16
  151.2 1.4 fusion.3
  152.6 1.1 copy-done.10
  153.8 1.7 multiply_reduce_fusion.1
  155.9 1.8 constant_dynamic-slice_fusion.1
  157.6 1.9 constant_dynamic-slice_fusion
  163.5 1.7 fusion.25
  165.2 1.9 concatenate.38
  167.1 37.0 %shard_map.163 = bf16[2,1024,896]{2,1,0:T(8,128)(2,1)} custom-call(bf16[2,128,896]{2,1,0:T(8,128)(2,1)} %bitcast.113), custom_call_target="tpu_custom_call" | custom-call | tf_op jit(solution)/shard_map/pallas_call | solution.py:511
  205.2 1.6 slice_add_fusion
  206.8 1.5 copy.48
  211.5 37.6 %shard_map.164 = (bf16[3,768,768]{2,1,0:T(8,128)(2,1)}, f32[256,768]{1,0:T(8,128)}) custom-call(bf16[2048,768]{1,0:T(8,128)(2,1)} %fusion.2.refs_0_, bf16[256,768]{1,0:T(8,128)(2,1)} %multiply_convert_fusion.2.refs_1_, bf16[768,2304]{1,0:T(8,128)(2,1)} %get-tuple-element.24.refs_2_.refs_3_.refs_4_, ...), custom_call_target="tpu_custom_call" | custom-call | flops 9865003008 | bytes 26214400 | tf_op jit(solution)/shard_map/pallas_call | solution.py:747
  249.1 1.5 multiply_reduce_fusion.3
  251.1 1.1 add_convert_fusion.1
  254.1 1.2 constant_dynamic-update-slice_fusion.6
  257.3 1.2 convolution_convert_fusion
  261.0 1.1 constant_dynamic-update-slice_fusion.2
  264.8 1.3 constant_dynamic-update-slice_fusion
  267.0 132.1 %shard_map.165 = bf16[1664,768]{1,0:T(8,128)(2,1)} custom-call(bf16[4,1664,768]{2,1,0:T(8,128)(2,1)} %pad_dynamic-update-slice_fusion.terms), custom_call_target="tpu_custom_call" | custom-call | tf_op jit(solution)/shard_map/pallas_call | solution.py:605
  399.1 2.7 fusion.52
  401.8 1.3 pad_maximum_fusion
  403.1 1.3 pad_maximum_fusion.1
  404.4 2.0 slice.149
  406.4 1.3 fusion.51
  (124 shorter events, 29.6 us)
Async XLA Ops:
  100.4 2.8 copy-start
  104.3 2.5 copy-start.1
  106.8 1.4 copy-start.25
  107.2 1.0 copy-start.23
  107.3 4.8 %copy-start.19 = (f32[256]{0:T(256)}, f32[256]{0:T(256)S(1)}, u32[]{:S(2)}) copy-start(f32[256]{0:T(256)S(1)} %bitcast_rsqrt_fusion) | copy-start | bytes 3076
  112.0 3.0 copy-start.27
  112.0 4.5 %copy-start.26 = (s32[2,128]{1,0:T(2,128)S(1)}, s32[2,128]{1,0:T(2,128)}, u32[]{:S(2)}) copy-start(s32[2,128]{1,0:T(2,128)} %param.18) | copy-start | bytes 3076
  117.9 24.4 %copy-start.7 = (bf16[768,768]{1,0:T(8,128)(2,1)S(1)}, bf16[768,768]{1,0:T(8,128)(2,1)}, u32[]{:S(2)}) copy-start(bf16[768,768]{1,0:T(8,128)(2,1)} %get-tuple-element.27) | copy-start | bytes 3538948
  144.4 11.2 %copy-start.17 = (f32[256]{0:T(256)}, f32[256]{0:T(256)S(1)}, u32[]{:S(2)}) copy-start(f32[256]{0:T(256)S(1)} %fusion.39) | copy-start | bytes 3076
  144.4 3.3 copy-start.11
  144.4 3.3 copy-start.13
  150.5 2.1 copy-start.14
  151.2 1.5 copy-start.5
  151.2 2.6 copy-start.10
  157.6 2.4 copy-start.8
  159.5 0.6 copy-start.21
  160.1 1.1 copy-start.3
  160.1 2.0 copy-start.16
  160.6 1.5 copy-start.12
  249.0 1.5 copy-start.24
  249.1 1.5 copy-start.2
  249.1 1.5 copy-start.20
  249.1 2.0 copy-start.22
  250.6 2.1 copy-start.9
  254.1 2.3 copy-start.18
  255.3 1.7 copy-start.6
  255.3 2.0 copy-start.15
  261.0 1.5 copy-start.4
  264.8 1.3 copy-start.28

commit v2 on v1

--- a/solution.py
+++ b/solution.py
@@ -514,6 +514,7 @@
         out_specs=[pl.BlockSpec(memory_space=pl.ANY)] * count,
         out_shape=[jax.ShapeDtypeStruct(shape, a.dtype) for shape, a in zip(shapes, arrays)],
         scratch_shapes=[dma((count,)), dma((count, 3)), dma((count, 3)), dma((count, 4)), dma((count, 4))],
+        cost_estimate=pl.CostEstimate(flops=0, bytes_accessed=120 * 1024 * 1024, transcendentals=0),
         compiler_params=pltpu.CompilerParams(collective_id=collective, has_side_effects=True),
     )(*arrays)
 
@@ -612,6 +613,7 @@
             pltpu.VMEM((half, width), bf), pltpu.VMEM((3, half // 4, width), bf), pltpu.VMEM((half // 4, width), bf),
             dma((4,)), dma((4,)), dma((3,)), dma((3,)), dma((3,)), dma((3,)), dma((3,)), dma((3,)), dma((3,)),
         ],
+        cost_estimate=pl.CostEstimate(flops=0, bytes_accessed=150 * 1024 * 1024, transcendentals=0),
         compiler_params=pltpu.CompilerParams(
             collective_id=collective, has_side_effects=True, vmem_limit_bytes=VMEM_LIMIT
         ),
@@ -781,20 +783,23 @@
 
     gain_rows = jnp.stack([grad_gain_attn, grad_gain_mlp]).reshape(2, dp_size, shard)
     gain_rows = jnp.pad(jnp.transpose(gain_rows, (1, 0, 2)), ((0, 0), (0, 0), (0, width - shard)))
-    stacked = [by_owner(dw_qkv[part]) for part in range(3)] + thirds(grad_in)
-    stacked += [by_owner(grad_attn_out), by_owner(grad_mix)]
-    used = sum(term.shape[1] for term in stacked)
+    early = jnp.concatenate(thirds(grad_in) + [by_owner(grad_attn_out), by_owner(grad_mix)], 1)
+    early = lax.psum_scatter(early, "dp", scatter_dimension=0, tiled=True)
+    stacked = [by_owner(dw_qkv[part]) for part in range(3)]
+    used = 3 * shard
     padded = -(-(used + 2) // 128) * 128
     stacked.append(jnp.pad(gain_rows.astype(bf), ((0, 0), (0, padded - used - 2), (0, 0))))
-    summed = reduce_terms(jnp.concatenate(stacked, 1), 2).astype(f32)
-    cuts = [summed[part * shard : (part + 1) * shard] for part in range(7)]
+    early, late = lax.optimization_barrier((early, jnp.concatenate(stacked, 1)))
+    early = lax.psum(early, "ctx")[0].astype(f32)
+    summed = reduce_terms(late, 2).astype(f32)
+    cuts = [early[part * shard : (part + 1) * shard] for part in range(4)]
     return (
         output.astype(bf).reshape(hidden_in.shape),
         grad_hidden,
+        jnp.concatenate([summed[part * shard : (part + 1) * shard] for part in range(3)], 1),
+        cuts[3],
         jnp.concatenate(cuts[:3], 1),
-        cuts[6],
-        jnp.concatenate(cuts[3:6], 1),
-        summed[7 * shard : used],
+        early[4 * shard :],
         summed[used, :shard],
         summed[used + 1, :shard],
     )

time: 413 us -> 410 us (level)
  Pallas kernels: 327 us -> 257 us
  waiting for transfers between devices: 0 us -> 58.7 us
  between operations: 1.13 us -> 14.6 us
  local copies, waits for them, and re-layouts: 35.9 us -> 26.6 us
  other arithmetic: 28.6 us -> 37.4 us
    pallas_call x1, Pallas kernels: 132 us -> 62.5 us  [reduce_terms(): pl.pallas_call(reduce_kernel, in_specs=[pl.BlockSpec(memory_space=pltpu.V...]
    psum x0 -> x1, waiting for transfers between devices: none -> 58.6 us  [body(): early = lax.psum(early, 'ctx')[0].astype(f32)]
    unnamed x67 -> x73, local copies, waits for them, and re-layouts: 14.1 us -> 10.1 us
  transfers between devices with their start and end apart: 0 -> 2, of which waited for: 0 -> 1; matrix products, arithmetic and copies ran while one was open for 0% -> 5% of each run, Pallas kernels for 0% -> 18%
where the time goes in v2:
time: 410 us; the launch traced here: 409 us
  Pallas kernels  257 us (63%)
  waiting for transfers between devices  58.7 us (14%)
  other arithmetic  37.4 us (9%)
  local copies, waits for them, and re-layouts  26.6 us (6%)
  between operations  14.6 us (4%)
  matrix products  14.4 us (4%)
    pallas_call x2, Pallas kernels, gather(): pl.pallas_call(lambda *refs: gather_kernel(n_dp, count - n_dp, *refs), in...  133 us
    pallas_call x1, Pallas kernels, reduce_terms(): pl.pallas_call(reduce_kernel, in_specs=[pl.BlockSpec(memory_space=pltpu.V...  62.5 us
    psum x1, waiting for transfers between devices, body(): early = lax.psum(early, 'ctx')[0].astype(f32)  58.6 us
    pallas_call x1, Pallas kernels, body(): pl.pallas_call(lambda *refs: backward_kernel(seqs, *refs), grid=(pairs,),...  37.4 us
    pallas_call x1, Pallas kernels, body(): pl.pallas_call(lambda *refs: forward_kernel(seqs, *refs), grid=(pairs,),...  24.4 us
    unnamed x73, local copies, waits for them, and re-layouts  10.1 us
  transfers between devices with their start and end apart: 2, of which 1 were waited for; matrix products, arithmetic and copies ran while one was open for 5% of the time, Pallas kernels for 18%

profile of v2, /device:TPU:0, one launch (start us, length us, event | category | flops | bytes accessed | tf_op | source)
XLA Modules:
  0.0 408.7 jit_solution(5522592656088195201)
XLA Ops:
  9.1 1.2 convert_bitcast_fusion
  11.6 1.1 convert_reduce_fusion.1
  13.3 95.7 %shard_map.161 = (bf16[768,2304]{1,0:T(8,128)(2,1)}, bf16[768,768]{1,0:T(8,128)(2,1)}, bf16[768,2304]{1,0:T(8,128)(2,1)}, bf16[1152,768]{1,0:T(8,128)(2,1)}, bf1...) custom-call(bf16[192,2304]{1,0:T(8,128)(2,1)} %refs_0_.1, bf16[192,768]{1,0:T(8,128)(2,1)} %refs_1_.1, ...), custom_call_target="tpu_custom_call" | custom-call | bytes 125829120 | tf_op jit(solution)/shard_map/pallas_call | solution.py:511
  110.4 2.5 convert_reduce_fusion
  116.4 5.7 %fusion.19 = (f32[2048,32]{1,0:T(8,128)}, f32[2048,32]{1,0:T(8,128)}, f32[2048,32]{1,0:T(8,128)}) fusion(f32[32]{0:T(128)S(1)} %copy-done.33, f32[2048]{0:T(1024)S(1)} %get-tuple-element.75), kind=kLoop, calls=%fused_computation.73 | loop fusion | flops 131072 | bytes 794752 | tf_op jit(solution)/shard_map/neg | solution.py:630
  122.1 1.3 fusion.28
  125.5 2.3 fusion.3.refs_0_
  128.8 3.0 pad_maximum_fusion.2
  133.5 24.4 %shard_map.162 = (bf16[256,768]{1,0:T(8,128)(2,1)}, bf16[2048,768]{1,0:T(8,128)(2,1)}, bf16[2048,768]{1,0:T(8,128)(2,1)}, f32[256,768]{1,0:T(8,128)}, f32[256,768]{1,0:T(8,128)}) custom-call(bf16[2048,768]{1,0:T(8,128)(2,1)} %fusion.3.refs_0_, bf16[256,768]{1,0:T(8,128)(2,1)} %multiply_convert_fusion.2.refs_1_, ...), custom_call_target="tpu_custom_call" | custom-call | flops 6442450944 | bytes 20971520 | tf_op jit(solution)/shard_map/pallas_call | solution.py:685
  158.0 1.8 fusion.56
  160.2 1.1 fusion.47
  161.8 2.8 fusion.18
  165.3 1.8 multiply_reduce_fusion.1
  167.0 1.2 convolution_convert_fusion
  174.6 1.1 constant_dynamic-update-slice_fusion.1
  175.7 1.4 constant_dynamic-update-slice_fusion
  177.2 1.6 fusion.17
  181.1 1.2 concatenate.41
  182.3 37.0 %shard_map.163 = bf16[2,1024,896]{2,1,0:T(8,128)(2,1)} custom-call(bf16[2,128,896]{2,1,0:T(8,128)(2,1)} %bitcast.124), custom_call_target="tpu_custom_call" | custom-call | bytes 125829120 | tf_op jit(solution)/shard_map/pallas_call | solution.py:511
  223.1 1.8 constant_dynamic-slice_fusion.1
  224.9 1.8 constant_dynamic-slice_fusion
  226.7 37.4 %shard_map.164 = (bf16[3,768,768]{2,1,0:T(8,128)(2,1)}, f32[256,768]{1,0:T(8,128)}) custom-call(bf16[2048,768]{1,0:T(8,128)(2,1)} %fusion.3.refs_0_, bf16[256,768]{1,0:T(8,128)(2,1)} %multiply_convert_fusion.2.refs_1_, bf16[768,2304]{1,0:T(8,128)(2,1)} %get-tuple-element.26.refs_2_.refs_3_.refs_4_, ...), custom_call_target="tpu_custom_call" | custom-call | flops 9865003008 | bytes 26214400 | tf_op jit(solution)/shard_map/pallas_call | solution.py:749
  264.1 1.5 multiply_reduce_fusion.3
  266.3 1.1 add_convert_fusion.1
  268.1 1.4 fusion.5
  270.4 2.1 fusion.4.terms
  272.5 62.5 %shard_map.165 = bf16[640,768]{1,0:T(8,128)(2,1)} custom-call(bf16[4,640,768]{2,1,0:T(8,128)(2,1)} %fusion.4.terms), custom_call_target="tpu_custom_call" | custom-call | bytes 157286400 | tf_op jit(solution)/shard_map/pallas_call | solution.py:606
  335.1 1.2 copy-done.2
  337.0 1.3 pad_maximum_fusion
  338.3 58.6 %all-reduce.9.cloned.1.call-done = bf16[1,1056,768]{2,1,0:T(8,128)(2,1)} async-done(((bf16[1,1056,768]{2,1,0:T(8,128)(2,1)}), bf16[1,1056,768]{2,1,0:T(8,128)(2,1)}) %all-reduce.9.cloned.1.call-update) | async-done | bytes 1622032 | tf_op jit(solution)/shard_map/psum | solution.py:793
  396.9 1.7 convert_element_type.141
  400.6 1.3 pad_maximum_fusion.1
  (139 shorter events, 32.0 us)
Async XLA Ops:
  7.2 265.4 %reduce-scatter.4.cloned.1.call-start = ((), (), s32[]{:S(2)}) async-start(), calls=%async_computation.2 | async-start | bytes 8110080
  110.4 2.8 copy-start
  113.3 2.2 copy-start.1
  113.3 3.1 copy-start.29
  113.3 3.1 copy-start.33
  115.8 6.4 %copy-start.27 = (f32[2,128]{1,0:T(2,128)}, f32[2,128]{1,0:T(2,128)S(1)}, u32[]{:S(2)}) copy-start(f32[2,128]{1,0:T(2,128)S(1)} %multiply_reduce_fusion.6) | copy-start | bytes 3076
  116.4 5.8 %copy-start.30 = (f32[256]{0:T(256)S(1)}, f32[256]{0:T(256)}, u32[]{:S(2)}) copy-start(f32[256]{0:T(256)} %convert_bitcast_fusion) | copy-start | bytes 3076
  125.5 2.3 copy-start.23
  125.5 2.3 copy-start.24
  125.5 3.3 copy-start.11
  125.5 3.3 copy-start.12
  125.5 3.3 copy-start.13
  128.7 3.1 copy-start.20
  128.7 3.0 copy-start.21
  128.7 3.0 copy-start.22
  128.8 4.0 copy-start.31
  133.5 24.4 %copy-start.10 = (bf16[768,768]{1,0:T(8,128)(2,1)S(1)}, bf16[768,768]{1,0:T(8,128)(2,1)}, u32[]{:S(2)}) copy-start(bf16[768,768]{1,0:T(8,128)(2,1)} %get-tuple-element.29) | copy-start | bytes 3538948
  157.9 2.2 copy-start.15
  160.2 1.6 copy-start.18
  165.3 6.4 %copy-start.8 = (bf16[256,1152]{1,0:T(8,128)(2,1)}, bf16[256,1152]{1,0:T(8,128)(2,1)S(1)}, u32[]{:S(2)}) copy-start(bf16[256,1152]{1,0:T(8,128)(2,1)S(1)} %get-tuple-element.59) | copy-start | bytes 1769476
  168.6 1.4 copy-start.6
  168.7 1.3 copy-start.25
  177.1 219.9 %all-reduce.9.cloned.1.call-start = ((), (), s32[]{:S(2)}) async-start(), calls=%async_computation.1 | async-start | bytes 3244032 | tf_op jit(solution)/shard_map/psum | solution.py:793
  179.3 3.0 copy-start.17
  221.1 1.9 copy-start.32
  264.1 1.6 copy-start.28
  264.1 1.6 copy-start.3
  264.1 2.1 copy-start.7
  264.1 2.1 copy-start.26
  266.3 1.8 copy-start.19
  268.1 2.1 copy-start.14
  335.1 1.2 copy-start.2
  (4 other events, 4.6 us)
Sparse Core Ops, SparseCore 0:
  177.2 70.1 reduce-scatter.3
  335.2 61.6 all-reduce.8

commit v3 on v2

--- a/solution.py
+++ b/solution.py
@@ -646,8 +646,11 @@
     shard = width // dp_size
     own_gains = jnp.pad(jnp.stack([attn_gain, mlp_gain]), ((0, 30), (0, 256 - shard)))
     own_marks = jnp.pad(jnp.concatenate([segment_ids, positions]), ((0, 8 - 2 * seqs), (0, 0)))
-    full_qkv, full_out, full_in, full_mix, gains, hidden_all, marks = gather(
-        [w_qkv, w_out, w_in, w_mix, own_gains], [hidden_in, own_marks.reshape(1, 8, local)], 0
+    full_out, full_in, full_mix = (
+        lax.all_gather(weight, "dp", axis=0, tiled=True) for weight in (w_out, w_in, w_mix)
+    )
+    full_qkv, gains, hidden_all, marks = gather(
+        [w_qkv, own_gains], [hidden_in, own_marks.reshape(1, 8, local)], 0
     )
     gains = gains.reshape(dp_size, 32, 256)[:, :2, :shard]
     gains = jnp.transpose(gains, (1, 0, 2)).reshape(2, width)

time: 410 us -> 380 us (0.927)
  Pallas kernels: 257 us -> 209 us
  waiting for transfers between devices: 58.7 us -> 79.7 us
  other arithmetic: 37.4 us -> 33.1 us
    pallas_call x2, Pallas kernels: 133 us -> 84 us  [gather(): pl.pallas_call(lambda *refs: gather_kernel(n_dp, count - n_dp, *refs), in...]
    all_gather x0 -> x3, waiting for transfers between devices: none -> 19.2 us  [body(): lax.all_gather(weight, 'dp', axis=0, tiled=True)]
    unnamed x73 -> x71, local copies, waits for them, and re-layouts: 10.1 us -> 11.1 us
  transfers between devices with their start and end apart: 2 -> 5, of which waited for: 1 -> 2; matrix products, arithmetic and copies ran while one was open for 5% -> 13% of each run, Pallas kernels for 18% -> 39%
where the time goes in v3:
time: 380 us; the launch traced here: 379 us
  Pallas kernels  209 us (55%)
  waiting for transfers between devices  79.7 us (21%)
  other arithmetic  33.1 us (9%)
  local copies, waits for them, and re-layouts  26.3 us (7%)
  matrix products  16.7 us (4%)
  between operations  14.4 us (4%)
    pallas_call x2, Pallas kernels, gather(): pl.pallas_call(lambda *refs: gather_kernel(n_dp, count - n_dp, *refs), in...  84 us
    pallas_call x1, Pallas kernels, reduce_terms(): pl.pallas_call(reduce_kernel, in_specs=[pl.BlockSpec(memory_space=pltpu.V...  62.3 us
    psum x1, waiting for transfers between devices, body(): early = lax.psum(early, 'ctx')[0].astype(f32)  58.4 us
    pallas_call x1, Pallas kernels, body(): pl.pallas_call(lambda *refs: backward_kernel(seqs, *refs), grid=(pairs,),...  38.4 us
    pallas_call x1, Pallas kernels, body(): pl.pallas_call(lambda *refs: forward_kernel(seqs, *refs), grid=(pairs,),...  24.3 us
    all_gather x3, waiting for transfers between devices, body(): lax.all_gather(weight, 'dp', axis=0, tiled=True)  19.2 us
    unnamed x71, local copies, waits for them, and re-layouts  11.1 us
  transfers between devices with their start and end apart: 5, of which 2 were waited for; matrix products, arithmetic and copies ran while one was open for 13% of the time, Pallas kernels for 39%

profile of v3, /device:TPU:0, one launch (start us, length us, event | category | flops | bytes accessed | tf_op | source)
XLA Modules:
  0.0 379.4 jit_solution(1522516307248389535)
XLA Ops:
  11.4 46.1 %shard_map.161 = (bf16[768,2304]{1,0:T(8,128)(2,1)}, bf16[128,256]{1,0:T(8,128)(2,1)}, bf16[2,1024,768]{2,1,0:T(8,128)(2,1)}, s32[1,64,128]{2,1,0:T(8,128)}) custom-call(bf16[192,2304]{1,0:T(8,128)(2,1)} %refs_0_.1, bf16[32,256]{1,0:T(8,128)(2,1)} %fusion.34.refs_1_, bf16[2,128,768]{2,1,0:T(8,128)(2,1)} %refs_2_.1, s32[1,8,128]{2,1,0:T(8,128)} %pad_bitcast_fusion.refs_3_), custom_call_target="tpu_custom_call" | custom-call | bytes 125829120 | tf_op jit(solution)/shard_map/pallas_call | solution.py:511
  58.9 2.5 convert_reduce_fusion
  63.2 3.7 fusion.19
  67.0 1.3 fusion.28
  69.2 3.0 pad_maximum_fusion.2
  74.2 2.6 pad_maximum_fusion.4
  76.7 3.1 fusion.3.refs_0_
  80.6 24.3 %shard_map.162 = (bf16[256,768]{1,0:T(8,128)(2,1)}, bf16[2048,768]{1,0:T(8,128)(2,1)}, bf16[2048,768]{1,0:T(8,128)(2,1)}, f32[256,768]{1,0:T(8,128)}, f32[256,768]{1,0:T(8,128)}) custom-call(bf16[2048,768]{1,0:T(8,128)(2,1)} %fusion.3.refs_0_, bf16[256,768]{1,0:T(8,128)(2,1)} %multiply_convert_fusion.2.refs_1_, ...), custom_call_target="tpu_custom_call" | custom-call | flops 6442450944 | bytes 20971520 | tf_op jit(solution)/shard_map/pallas_call | solution.py:688
  104.9 2.2 fusion.56
  107.9 3.1 fusion.47
  111.1 19.2 %all-gather.8.cloned.1.call-done = bf16[1152,768]{1,0:T(8,128)(2,1)} async-done(((bf16[288,768]{1,0:T(8,128)(2,1)}), bf16[1152,768]{1,0:T(8,128)(2,1)}) %all-gather.8.cloned.1.call-update) | async-done | bytes 1769488 | tf_op jit(solution)/shard_map/all_gather | solution.py:650
  130.2 4.4 %fusion.18 = (f32[256,1152]{1,0:T(8,128)S(1)}, f32[256,1152]{1,0:T(8,128)S(1)}, f32[256,1152]{1,0:T(8,128)S(1)}) fusion(f32[256,2304]{1,0:T(8,128)S(1)} %fusion.47, bf16[256,768]{1,0:T(8,128)(2,1)} %bitcast.120, bf16[1152,768]{1,0:T(8,128)(2,1)} %all-gather.8.cloned.1.call-done), kind=kOutput, calls=%fused_computation.71 | convolution fusion | flops 472154112 | bytes 6881280 | tf_op jit(solution)/shard_map/dot_general | solution.py:48
  135.3 1.2 convolution_convert_fusion
  137.5 1.2 multiply_reduce_fusion.1
  139.4 1.1 constant_dynamic-update-slice_fusion.4
  144.0 1.1 constant_dynamic-update-slice_fusion.2
  146.2 1.4 constant_dynamic-update-slice_fusion
  147.7 1.9 constant_dynamic-slice_fusion.1
  149.6 1.8 constant_dynamic-slice_fusion
  154.2 1.2 concatenate.41
  155.4 37.9 %shard_map.163 = bf16[2,1024,896]{2,1,0:T(8,128)(2,1)} custom-call(bf16[2,128,896]{2,1,0:T(8,128)(2,1)} %bitcast.122), custom_call_target="tpu_custom_call" | custom-call | bytes 125829120 | tf_op jit(solution)/shard_map/pallas_call | solution.py:511
  197.0 38.4 %shard_map.164 = (bf16[3,768,768]{2,1,0:T(8,128)(2,1)}, f32[256,768]{1,0:T(8,128)}) custom-call(bf16[2048,768]{1,0:T(8,128)(2,1)} %fusion.3.refs_0_, bf16[256,768]{1,0:T(8,128)(2,1)} %multiply_convert_fusion.2.refs_1_, bf16[768,2304]{1,0:T(8,128)(2,1)} %get-tuple-element.23.refs_2_.refs_3_.refs_4_, ...), custom_call_target="tpu_custom_call" | custom-call | flops 9865003008 | bytes 26214400 | tf_op jit(solution)/shard_map/pallas_call | solution.py:752
  235.5 1.5 multiply_reduce_fusion.3
  237.6 1.1 add_convert_fusion.1
  239.4 1.4 fusion.5
  241.8 2.1 fusion.4.terms
  243.9 62.3 %shard_map.165 = bf16[640,768]{1,0:T(8,128)(2,1)} custom-call(bf16[4,640,768]{2,1,0:T(8,128)(2,1)} %fusion.4.terms), custom_call_target="tpu_custom_call" | custom-call | bytes 157286400 | tf_op jit(solution)/shard_map/pallas_call | solution.py:606
  306.3 1.2 copy-done.3
  308.2 1.3 pad_maximum_fusion
  309.5 58.4 %all-reduce.9.cloned.1.call-done = bf16[1,1056,768]{2,1,0:T(8,128)(2,1)} async-done(((bf16[1,1056,768]{2,1,0:T(8,128)(2,1)}), bf16[1,1056,768]{2,1,0:T(8,128)(2,1)}) %all-reduce.9.cloned.1.call-update) | async-done | bytes 1622032 | tf_op jit(solution)/shard_map/psum | solution.py:796
  367.9 1.7 convert_element_type.141
  371.5 1.3 pad_maximum_fusion.1
  (146 shorter events, 29.8 us)
Async XLA Ops:
  7.2 2.8 copy-start.31
  7.2 2.8 copy-start.32
  7.2 2.8 copy-start.29
  7.2 2.9 copy-start.27
  7.2 3.5 copy-start.1
  7.2 97.7 %all-gather.4.cloned.1.call-start = ((), (), s32[]{:S(2)}) async-start(), calls=%async_computation.1 | async-start | bytes 1474560 | tf_op jit(solution)/shard_map/all_gather | solution.py:650
  8.0 100.0 %all-gather.6.cloned.1.call-start = ((), (), s32[]{:S(2)}) async-start(), calls=%async_computation.2 | async-start | bytes 4423680 | tf_op jit(solution)/shard_map/all_gather | solution.py:650
  8.7 121.5 %all-gather.8.cloned.1.call-start = ((), (), s32[]{:S(2)}) async-start(), calls=%async_computation.3 | async-start | bytes 2211840 | tf_op jit(solution)/shard_map/all_gather | solution.py:650
  9.4 234.5 %reduce-scatter.4.cloned.1.call-start = ((), (), s32[]{:S(2)}) async-start(), calls=%async_computation.5 | async-start | bytes 8110080
  58.9 2.8 copy-start
  61.8 1.4 copy-start.26
  61.8 1.4 copy-start.30
  62.9 5.4 %copy-start.18 = (f32[256]{0:T(256)}, f32[256]{0:T(256)S(1)}, u32[]{:S(2)}) copy-start(f32[256]{0:T(256)S(1)} %get-tuple-element.78) | copy-start | bytes 3076
  63.1 3.8 %copy-start.22 = (f32[2,128]{1,0:T(2,128)}, f32[2,128]{1,0:T(2,128)S(1)}, u32[]{:S(2)}) copy-start(f32[2,128]{1,0:T(2,128)S(1)} %multiply_reduce_fusion.6) | copy-start | bytes 3076
  63.2 5.1 %copy-start.20 = (f32[256]{0:T(256)}, f32[256]{0:T(256)S(1)}, u32[]{:S(2)}) copy-start(f32[256]{0:T(256)S(1)} %bitcast_rsqrt_fusion) | copy-start | bytes 3076
  76.7 3.1 copy-start.28
  135.3 6.9 %copy-start.9 = (bf16[256,1152]{1,0:T(8,128)(2,1)}, bf16[256,1152]{1,0:T(8,128)(2,1)S(1)}, u32[]{:S(2)}) copy-start(bf16[256,1152]{1,0:T(8,128)(2,1)S(1)} %get-tuple-element.53) | copy-start | bytes 1769476
  135.3 2.2 copy-start.13
  137.5 1.2 copy-start.25
  139.1 1.4 copy-start.7
  147.6 3.8 %copy-start.17 = (f32[256,768]{1,0:T(8,128)S(1)}, f32[256,768]{1,0:T(8,128)}, u32[]{:S(2)}) copy-start(f32[256,768]{1,0:T(8,128)} %get-tuple-element.29.refs_19_) | copy-start | bytes 2359300
  147.6 220.3 %all-reduce.9.cloned.1.call-start = ((), (), s32[]{:S(2)}) async-start(), calls=%async_computation.4 | async-start | bytes 3244032 | tf_op jit(solution)/shard_map/psum | solution.py:796
  147.7 4.2 %copy-start.11 = (bf16[768,768]{1,0:T(8,128)(2,1)S(1)}, bf16[768,768]{1,0:T(8,128)(2,1)}, u32[]{:S(2)}) copy-start(bf16[768,768]{1,0:T(8,128)(2,1)} %all-gather.4.cloned.1.call-done) | copy-start | bytes 3538948
  152.4 3.0 copy-start.15
  197.0 38.4 %copy-start.19 = (f32[256]{0:T(256)S(1)}, f32[256]{0:T(256)}, u32[]{:S(2)}) copy-start(f32[256]{0:T(256)} %copy-done.18) | copy-start | bytes 3076
  235.4 1.6 copy-start.23
  235.4 1.6 copy-start.4
  235.4 1.6 copy-start.21
  235.5 2.1 copy-start.8
  237.6 1.8 copy-start.16
  239.4 2.1 copy-start.12
  306.3 1.2 copy-start.3
  (6 other events, 6.2 us)
Sparse Core Ops, SparseCore 0:
  9.9 38.5 all-gather.3
  50.3 45.3 all-gather.5
  97.6 32.5 all-gather.7
  147.7 71.9 reduce-scatter.3
  306.4 61.4 all-reduce.8
